TPU v7x, 512 devices: a whole 4x4x16 slice. The times are simulated.
512 devices in a mesh: text: 16 (over y, x), graph: 32 (over z, core).
Axes of the slice: x: 4, y: 4, z: 16, core: 2. Of those that a mesh axis runs over, the one named last changes fastest.
Arguments:
- tokens: bfloat16 [262144, 768], P(('text', 'graph')), may hold values from -6 to 6
- doc_ids: int32 [2048, 128], P(('text', 'graph')), may hold values from 0 to 3, never falling along the last dimension, each value on 1 to 96 neighbouring positions
- in_gain: float32 [768], replicated, may hold values from 0.25 to 1.75
- in_bias: float32 [768], replicated, may hold values from -3 to 3
- attn_qkv: bfloat16 [768, 2304], P(None, 'text'), may hold values from -0.21875 to 0.21875
- attn_out: bfloat16 [768, 768], P(None, 'text'), may hold values from -0.21875 to 0.21875
- owner_text: int32 [8192, 1], P(('text', 'graph')), may hold values from 0 to 15; in each aligned block of 16 rows (0 to 15, 16 to 31, ...) at most 2 rows name the same one
- sage_one: bfloat16 [1536, 768], P('graph'), may hold values from -0.21875 to 0.21875
- sage_two: bfloat16 [1536, 768], P('graph'), may hold values from -0.21875 to 0.21875
- neighbours: int32 [16384, 15], P(('text', 'graph')), may hold values from 0 to 95
- boundary: int32 [16384, 2], P(('text', 'graph')), may hold values from 0 to 31
- out_grad: bfloat16 [16384, 768], P(('text', 'graph')), may hold values from -6 to 6
Outputs:
- node_states: bfloat16 [16384, 768], P(('text', 'graph'))
- abstract_grad: bfloat16 [8192, 768], P(('text', 'graph'))
Inputs may be any that keep to these rules, and one draw needn't show every extreme that they name: `doc_ids`: within each row the numbers never fall; each of the 4 numbers covers 1 to 96 positions. `owner_text`: among the 16 rows of one device no value occurs more than 2 times.
All inputs are finite; a program needn't handle non-finite values.
Results may differ from a plain program's by a relative error of at most 0.01.
Values may be sent and summed in bfloat16 or wider, within the bound.
A program may use at most 64 MiB of HBM per device.

v0:
```python
import math

import jax
import jax.numpy as jnp
from jax import lax
from jax.sharding import Mesh
from jax.sharding import PartitionSpec as P

HEAD = 64
SEGS = 4
TEXT = ("text_0", "text_1")
TEXT_GRAPH = ("text_0", "text_1", "graph")


epsilon = 1e-06
highest = lax.Precision.HIGHEST


def whole_of(x, axes, dim):
    if not axes:
        return x
    nearer = lax.all_gather(x, axes[-1], axis=dim, tiled=True)
    return whole_of(nearer, axes[:-1], dim)


def joined_along(tiles, dim):
    tiles = jnp.moveaxis(tiles, 0, dim)
    lengths = tiles.shape
    return tiles.reshape(*lengths[:dim], lengths[dim] * lengths[dim + 1], *lengths[dim + 2 :])


def from_everyone(x, axis):
    peers = lax.axis_size(axis)
    return lax.all_to_all(jnp.broadcast_to(x[None], (peers, *x.shape)), axis, 0, 0, tiled=True)


def gathered_copies(x, axis, dim):
    return joined_along(from_everyone(x, axis), dim)


def sent_together(arrays, axis, split_dim, concat_dim, along):
    widths = [math.prod(a.shape[along:]) for a in arrays]
    both = jnp.concatenate(
        [a.reshape(*a.shape[:along], w) for a, w in zip(arrays, widths)], axis=along
    )
    result = lax.all_to_all(both, axis, split_axis=split_dim, concat_axis=concat_dim, tiled=True)
    tiles = jnp.split(result, [sum(widths[:k]) for k in range(1, len(widths))], axis=along)
    return tuple(
        (b.reshape(*result.shape[:along], *a.shape[along:]) for a, b in zip(arrays, tiles))
    )


def sent_together_2(arrays, axis, dim, along):
    ends, at = ([], 0)
    for a in arrays[:-1]:
        at += a.shape[along]
        ends.append(at)
    both = jnp.concatenate(arrays, axis=along)
    return tuple(jnp.split(lax.all_gather(both, axis, axis=dim, tiled=True), ends, axis=along))


def layer_norm(tokens, in_gain, in_bias):
    states = tokens.astype(jnp.float32)
    row_mean = jnp.mean(states, axis=1, keepdims=True)
    centred = states - row_mean
    variance = jnp.mean(centred * centred, axis=1, keepdims=True)
    return (centred * lax.rsqrt(variance + epsilon) * in_gain + in_bias).astype(jnp.bfloat16)


def aggregate(hidden, halo_part, adjacency, weight, fan_out):
    width = hidden.shape[1]
    extended = jnp.concatenate([hidden, halo_part], axis=0)
    aggregated = (
        jnp.dot(adjacency, extended, preferred_element_type=jnp.float32) / fan_out
    ).astype(jnp.bfloat16)
    return jnp.dot(hidden, weight[:width], preferred_element_type=jnp.float32) + jnp.dot(
        aggregated, weight[width:], preferred_element_type=jnp.float32
    )


def spread_back(combined, adjacency, width, fan_out):
    row_count = combined.shape[0]
    self_part = combined[:, :width]
    spread = (combined[:, width:] / fan_out).astype(jnp.bfloat16)
    ext_grad = lax.dot_general(
        adjacency, spread, (((0,), (0,)), ((), ())), preferred_element_type=jnp.float32
    )
    return (self_part + ext_grad[:row_count], ext_grad[row_count:].astype(jnp.bfloat16))


def local(
    tokens,
    doc_ids,
    in_gain,
    in_bias,
    attn_qkv,
    attn_out,
    owner_text,
    sage_one,
    sage_two,
    neighbours,
    boundary,
    out_grad,
):
    width = tokens.shape[1]
    blocks, block_len = doc_ids.shape
    head_count = width // HEAD
    normed = layer_norm(tokens, in_gain, in_bias)
    projected = jnp.dot(
        normed, whole_of(attn_qkv, TEXT, 1), preferred_element_type=jnp.float32
    ).astype(jnp.bfloat16)
    projected = projected.reshape(blocks, block_len, 3, head_count, HEAD)
    scores = jnp.einsum(
        "bqhd,bkhd->bhqk",
        projected[:, :, 0],
        projected[:, :, 1],
        preferred_element_type=jnp.float32,
    ) * HEAD ** (-0.5)
    same_doc = doc_ids[:, None, :, None] == doc_ids[:, None, None, :]
    weights = jnp.where(same_doc, jnp.exp(scores), 0.0)
    probabilities = (weights / jnp.sum(weights, axis=3, keepdims=True)).astype(jnp.bfloat16)
    context = jnp.einsum(
        "bhqk,bkhd->bqhd", probabilities, projected[:, :, 2], preferred_element_type=jnp.float32
    )
    context = context.astype(jnp.bfloat16).reshape(blocks * block_len, width)
    node_total = blocks * SEGS
    node_of = (doc_ids + SEGS * jnp.arange(blocks, dtype=jnp.int32)[:, None]).reshape(-1)
    member = (node_of[None, :] == jnp.arange(node_total, dtype=jnp.int32)[:, None]).astype(
        jnp.bfloat16
    )
    lengths = jnp.sum(member.astype(jnp.float32), axis=1, keepdims=True)
    pooled_norm = jnp.dot(member, normed, preferred_element_type=jnp.float32)
    pooled_context = jnp.dot(member, context, preferred_element_type=jnp.float32)
    total = pooled_norm + jnp.dot(
        pooled_context, gathered_copies(attn_out, TEXT, 1).astype(jnp.float32), precision=highest
    )
    embedded = (total / lengths).astype(jnp.bfloat16)
    text_count = lax.axis_size(TEXT)
    graph_count = lax.axis_size("graph")
    row_count = out_grad.shape[0]
    capacity = row_count // text_count
    targets = owner_text[:, 0]
    positions = jnp.arange(node_total, dtype=jnp.int32)
    earlier = (positions[None, :] < positions[:, None]) & (targets[None, :] == targets[:, None])
    slot_index = targets * capacity + jnp.sum(earlier.astype(jnp.int32), axis=1)
    slots = (slot_index[:, None] == jnp.arange(row_count, dtype=jnp.int32)[None, :]).astype(
        jnp.bfloat16
    )
    outgoing = lax.dot_general(
        slots, embedded, (((0,), (0,)), ((), ())), preferred_element_type=jnp.float32
    ).astype(jnp.bfloat16)
    filled = jnp.sum(slots.astype(jnp.float32), axis=0).astype(jnp.bfloat16)
    arrived, alive = sent_together(
        (outgoing.reshape(text_count, capacity, width), filled.reshape(text_count, capacity)),
        TEXT,
        0,
        0,
        2,
    )
    node_rows = arrived.reshape(row_count, width)
    live_half = alive.reshape(row_count, 1)
    live_rows = live_half.astype(jnp.float32)
    slot_count = boundary.shape[1]
    halo_count = graph_count * slot_count
    extent = row_count + halo_count
    fan_out = neighbours.shape[1]
    adjacency = jnp.sum(
        (neighbours[:, :, None] == jnp.arange(extent, dtype=jnp.int32)[None, None, :]).astype(
            jnp.float32
        ),
        axis=1,
    ).astype(jnp.bfloat16)
    picker = (
        boundary.reshape(-1)[:, None] == jnp.arange(row_count, dtype=jnp.int32)[None, :]
    ).astype(jnp.bfloat16)

    def trade(hidden):
        leaving = jnp.dot(picker, hidden, preferred_element_type=jnp.float32).astype(jnp.bfloat16)
        coming = lax.all_to_all(
            leaving.reshape(graph_count, slot_count, width),
            "graph",
            split_axis=0,
            concat_axis=0,
            tiled=True,
        )
        return coming.reshape(halo_count, width)

    def give_back(halo_grad):
        coming = lax.all_to_all(
            halo_grad.reshape(graph_count, slot_count, width),
            "graph",
            split_axis=0,
            concat_axis=0,
            tiled=True,
        )
        return lax.dot_general(
            picker,
            coming.reshape(halo_count, width),
            (((0,), (0,)), ((), ())),
            preferred_element_type=jnp.float32,
        )

    layer_one, layer_two = sent_together_2((sage_one, sage_two), "graph", 0, 1)
    preact_one = aggregate(node_rows, trade(node_rows), adjacency, layer_one, fan_out)
    hidden_one = (live_rows * jax.nn.gelu(preact_one)).astype(jnp.bfloat16)
    preact_two = aggregate(hidden_one, trade(hidden_one), adjacency, layer_two, fan_out)
    node_states = (live_rows * preact_two).astype(jnp.bfloat16)

    def transposed(gradient, whole):
        return lax.dot_general(
            gradient, whole, (((1,), (1,)), ((), ())), preferred_element_type=jnp.float32
        )

    grad_two = out_grad * live_half
    local_two, halo_two = spread_back(transposed(grad_two, layer_two), adjacency, width, fan_out)
    into_one = local_two + give_back(halo_two)
    gelu_value, pull_back = jax.vjp(jax.nn.gelu, preact_one)
    grad_one = (live_rows * pull_back(into_one)[0]).astype(jnp.bfloat16)
    local_one, halo_one = spread_back(transposed(grad_one, layer_one), adjacency, width, fan_out)
    embed_grad = (local_one + give_back(halo_one)).astype(jnp.bfloat16)
    returned = lax.all_to_all(
        embed_grad.reshape(text_count, capacity, width),
        TEXT,
        split_axis=0,
        concat_axis=0,
        tiled=True,
    )
    abstract_grad = jnp.dot(
        slots, returned.reshape(row_count, width), preferred_element_type=jnp.float32
    ).astype(jnp.bfloat16)
    return (node_states, abstract_grad)


def solution(mesh):
    torus = Mesh(mesh.devices.reshape(4, 4, mesh.shape["graph"]), ("text_0", "text_1", "graph"))
    placed = (
        P(TEXT_GRAPH, None),
        P(TEXT_GRAPH, None),
        P(),
        P(),
        P(None, TEXT),
        P(None, TEXT),
        P(TEXT_GRAPH, None),
        P("graph", None),
        P("graph", None),
        P(TEXT_GRAPH, None),
        P(TEXT_GRAPH, None),
        P(TEXT_GRAPH, None),
    )
    return jax.shard_map(
        local,
        mesh=torus,
        in_specs=placed,
        out_specs=(P(TEXT_GRAPH, None), P(TEXT_GRAPH, None)),
        check_vma=False,
    )
```

profile of v0, /device:TPU:1, one launch (start us, length us, event | category | flops | bytes accessed | tf_op | source)
XLA Modules:
  0.0 244.7 jit_solution(7779667678152687817)
XLA Ops:
  7.2 14.3 %all_gather.9 = bf16[768,576]{0,1:T(8,128)(2,1)} all-gather(bf16[768,144]{0,1:T(8,128)(2,1)} %param.16), channel_id=1, replica_groups=mesh['text_0'=4,'text_1'=4,'graph'=32] {'text_1'}, dimensions={1}, use_global_device_ids=true | all-gather | bytes 1105920 | tf_op jit(solution)/shard_map/all_gather | solution.py:22
  21.6 1.7 pad_maximum_fusion
  23.3 1.1 broadcast_in_dim.16
  24.4 5.4 %all-to-all-start = ((bf16[16,768,48]{1,2,0:T(8,128)(2,1)}), bf16[16,768,48]{1,2,0:T(8,128)(2,1)S(1)}, u32[]{:S(2)}, u32[]{:S(2)}) async-start(bf16[16,768,48]{1,2,0:T(8,128)(2,1)} %broadcast_in_dim.16), calls=%async_computation | async-start | bytes 2359296 | tf_op jit(solution)/shard_map/all_to_all | solution.py:34
  31.8 1.1 fusion.86
  32.9 46.1 %all-gather.3.cloned.1.call-done = bf16[768,2304]{0,1:T(8,128)(2,1)} async-done(((bf16[768,576]{0,1:T(8,128)(2,1)}), bf16[768,2304]{0,1:T(8,128)(2,1)}) %all-gather.3.cloned.1.call-update) | async-done | bytes 3538960 | tf_op jit(solution)/shard_map/all_gather | solution.py:22
  79.0 5.6 %convolution_convert_fusion = bf16[512,2304]{1,0:T(8,128)(2,1)} fusion(bf16[768,2304]{0,1:T(8,128)(2,1)} %all-gather.3.cloned.1.call-done, bf16[512,768]{1,0:T(8,128)(2,1)S(1)} %copy-done, f32[768]{0:T(1024)S(1)} %copy-done.10, f32[768]{0:T(1024)S(1)} %copy-done.11, f32[512]{0:T(512)S(1)} %add_rsqrt_fusion, f32[512]{0:T(512)S(1)} %broadcast_multiply_fusion), kind=kOutput, calls=%fused_computation | convolution fusion | flops 1815478272 | bytes 6694912 | tf_op jit(solution)/shard_map/dot_general | solution.py:109
  84.6 4.3 %copy.32 = bf16[512,2304]{0,1:T(8,128)(2,1)} copy(bf16[512,2304]{1,0:T(8,128)(2,1)} %convolution_convert_fusion) | data formatting | bytes 4718592 | tf_op jit(solution)/shard_map/convert_element_type | solution.py:111
  88.9 4.2 %reshape.92 = bf16[4,128,3,12,64]{1,0,4,3,2:T(4,128)(2,1)S(1)} reshape(bf16[512,2304]{0,1:T(8,128)(2,1)} %copy.32) | data formatting | bytes 4718592 | tf_op jit(solution)/shard_map/reshape | solution.py:112
  93.1 1.0 fusion.119
  94.2 1.0 fusion
  95.1 0.8 fusion.14
  97.0 1.0 fusion.39
  99.0 4.7 %all-to-all-start.1 = ((bf16[16,2,769]{2,1,0:T(2,128)(2,1)}), bf16[16,2,769]{2,1,0:T(2,128)(2,1)S(1)}, u32[]{:S(2)}, u32[]{:S(2)}) async-start(bf16[16,2,769]{2,1,0:T(2,128)(2,1)} %pad_maximum_fusion.1), calls=%async_computation.1 | async-start | bytes 114688 | tf_op jit(solution)/shard_map/all_to_all | solution.py:46
  104.0 6.3 %all-to-all-done.1 = bf16[16,2,769]{2,1,0:T(2,128)(2,1)S(1)} async-done(((bf16[16,2,769]{2,1,0:T(2,128)(2,1)}), bf16[16,2,769]{2,1,0:T(2,128)(2,1)S(1)}, u32[]{:S(2)}, u32[]{:S(2)}) %all-to-all-start.1) | async-done | bytes 49248 | tf_op jit(solution)/shard_map/all_to_all | solution.py:46
  111.2 14.4 %all-to-all-start.2 = ((bf16[32,2,768]{2,1,0:T(2,128)(2,1)}), bf16[32,2,768]{2,1,0:T(2,128)(2,1)S(1)}, u32[]{:S(2)}, u32[]{:S(2)}) async-start(bf16[32,2,768]{2,1,0:T(2,128)(2,1)} %reshape.97), calls=%async_computation.2 | async-start | bytes 196608 | tf_op jit(solution)/shard_map/all_to_all | solution.py:179
  126.0 15.9 %all-to-all-done.2 = bf16[32,2,768]{2,1,0:T(2,128)(2,1)S(1)} async-done(((bf16[32,2,768]{2,1,0:T(2,128)(2,1)}), bf16[32,2,768]{2,1,0:T(2,128)(2,1)S(1)}, u32[]{:S(2)}, u32[]{:S(2)}) %all-to-all-start.2) | async-done | bytes 98336 | tf_op jit(solution)/shard_map/all_to_all | solution.py:179
  141.9 16.8 %all-gather.5.cloned.1.call-done = bf16[1536,1536]{1,0:T(8,128)(2,1)} async-done(((bf16[48,1536]{1,0:T(8,128)(2,1)}), bf16[1536,1536]{1,0:T(8,128)(2,1)}) %all-gather.5.cloned.1.call-update) | async-done | bytes 4718608 | tf_op jit(solution)/shard_map/all_gather | solution.py:59
  158.8 2.4 fusion.3
  162.2 8.0 %all-to-all-start.4 = ((bf16[32,2,768]{2,1,0:T(2,128)(2,1)}), bf16[32,2,768]{2,1,0:T(2,128)(2,1)S(1)}, u32[]{:S(2)}, u32[]{:S(2)}) async-start(bf16[32,2,768]{2,1,0:T(2,128)(2,1)} %reshape.101), calls=%async_computation.4 | async-start | bytes 196608 | tf_op jit(solution)/shard_map/all_to_all | solution.py:189
  170.2 1.7 fusion.19
  171.8 1.6 multiply_convert_fusion
  174.4 10.4 %all-to-all-done.4 = bf16[32,2,768]{2,1,0:T(2,128)(2,1)S(1)} async-done(((bf16[32,2,768]{2,1,0:T(2,128)(2,1)}), bf16[32,2,768]{2,1,0:T(2,128)(2,1)S(1)}, u32[]{:S(2)}, u32[]{:S(2)}) %all-to-all-start.4) | async-done | bytes 98336 | tf_op jit(solution)/shard_map/all_to_all | solution.py:189
  184.8 5.0 %all-to-all-start.3 = ((bf16[32,2,768]{2,1,0:T(2,128)(2,1)}), bf16[32,2,768]{2,1,0:T(2,128)(2,1)S(1)}, u32[]{:S(2)}, u32[]{:S(2)}) async-start(bf16[32,2,768]{2,1,0:T(2,128)(2,1)} %reshape.99), calls=%async_computation.3 | async-start | bytes 196608 | tf_op jit(solution)/shard_map/all_to_all | solution.py:179
  189.8 2.7 %fusion.1 = f32[32,1536]{1,0:T(8,128)S(1)} fusion(bf16[1536,1536]{1,0:T(8,128)(2,1)} %all-gather.5.cloned.1.call-done, f32[32,768]{1,0:T(8,128)S(1)} %get-tuple-element.8, bf16[64,768]{1,0:T(8,128)(2,1)S(1)} %reshape.102, f32[96,768]{1,0:T(8,128)S(1)} %fusion.69, f32[32,1536]{1,0:T(8,128)S(1)} %fusion.3, f32[32]{0:T(128)S(1)} %convert_element_type.101, ...), kind=kOutput, calls=%fused_computation.4 | convolution fusion | flops 79210496 | bytes 2950144 | tf_op jit(solution)/shard_map/dot_general | solution.py:210
  193.4 10.6 %all-to-all-done.3 = bf16[32,2,768]{2,1,0:T(2,128)(2,1)S(1)} async-done(((bf16[32,2,768]{2,1,0:T(2,128)(2,1)}), bf16[32,2,768]{2,1,0:T(2,128)(2,1)S(1)}, u32[]{:S(2)}, u32[]{:S(2)}) %all-to-all-start.3) | async-done | bytes 98336 | tf_op jit(solution)/shard_map/all_to_all | solution.py:179
  204.0 5.3 %all-to-all-start.5 = ((bf16[32,2,768]{2,1,0:T(2,128)(2,1)}), bf16[32,2,768]{2,1,0:T(2,128)(2,1)S(1)}, u32[]{:S(2)}, u32[]{:S(2)}) async-start(bf16[32,2,768]{2,1,0:T(2,128)(2,1)} %reshape.103), calls=%async_computation.5 | async-start | bytes 196608 | tf_op jit(solution)/shard_map/all_to_all | solution.py:189
  209.4 1.7 fusion.15
  211.1 12.6 %all-to-all-done.5 = bf16[32,2,768]{2,1,0:T(2,128)(2,1)S(1)} async-done(((bf16[32,2,768]{2,1,0:T(2,128)(2,1)}), bf16[32,2,768]{2,1,0:T(2,128)(2,1)S(1)}, u32[]{:S(2)}, u32[]{:S(2)}) %all-to-all-start.5) | async-done | bytes 98336 | tf_op jit(solution)/shard_map/all_to_all | solution.py:189
  224.6 6.0 %all-to-all-start.6 = ((bf16[16,2,768]{2,1,0:T(2,128)(2,1)}), bf16[16,2,768]{2,1,0:T(2,128)(2,1)S(1)}, u32[]{:S(2)}, u32[]{:S(2)}) async-start(bf16[16,2,768]{2,1,0:T(2,128)(2,1)} %reshape.105), calls=%async_computation.6 | async-start | bytes 98304 | tf_op jit(solution)/shard_map/all_to_all | solution.py:221
  230.6 2.2 fusion.32
  232.8 4.2 %all-to-all-done.6 = bf16[16,2,768]{2,1,0:T(2,128)(2,1)S(1)} async-done(((bf16[16,2,768]{2,1,0:T(2,128)(2,1)}), bf16[16,2,768]{2,1,0:T(2,128)(2,1)S(1)}, u32[]{:S(2)}, u32[]{:S(2)}) %all-to-all-start.6) | async-done | bytes 49184 | tf_op jit(solution)/shard_map/all_to_all | solution.py:221
  (74 shorter events, 10.2 us)
Async XLA Ops:
  7.2 16.1 %copy-start.1 = (bf16[768,48]{0,1:T(8,128)(2,1)S(1)}, bf16[768,48]{0,1:T(8,128)(2,1)}, u32[]{:S(2)}) copy-start(bf16[768,48]{0,1:T(8,128)(2,1)} %param.17) | copy-start | bytes 221188
  7.2 71.9 %all-gather.3.cloned.1.call-start = ((), (), s32[]{:S(2)}) async-start(), calls=%async_computation.7 | async-start | bytes 4423680 | tf_op jit(solution)/shard_map/all_gather | solution.py:22
  21.5 8.3 %copy-start.12 = (s32[16,1]{0,1:T(1,128)S(1)}, s32[16,1]{0,1:T(1,128)}, u32[]{:S(2)}) copy-start(s32[16,1]{0,1:T(1,128)} %param.18) | copy-start | bytes 196
  21.5 8.7 %copy-start.5 = (s32[4,128]{1,0:T(4,128)S(1)}, s32[4,128]{1,0:T(4,128)}, u32[]{:S(2)}) copy-start(s32[4,128]{1,0:T(4,128)} %param.13) | copy-start | bytes 6148
  21.5 9.0 %copy-start = (bf16[512,768]{1,0:T(8,128)(2,1)S(1)}, bf16[512,768]{1,0:T(8,128)(2,1)}, u32[]{:S(2)}) copy-start(bf16[512,768]{1,0:T(8,128)(2,1)} %param.12) | copy-start | bytes 2359300
  21.5 137.2 %all-gather.5.cloned.1.call-start = ((), (), s32[]{:S(2)}) async-start(), calls=%async_computation.8 | async-start | bytes 4866048 | tf_op jit(solution)/shard_map/all_gather | solution.py:59
  23.3 8.5 %copy-start.10 = (f32[768]{0:T(1024)S(1)}, f32[768]{0:T(1024)}, u32[]{:S(2)}) copy-start(f32[768]{0:T(1024)} %param.15) | copy-start | bytes 9220
  23.3 8.5 %copy-start.11 = (f32[768]{0:T(1024)S(1)}, f32[768]{0:T(1024)}, u32[]{:S(2)}) copy-start(f32[768]{0:T(1024)} %param.14) | copy-start | bytes 9220
  24.4 72.6 %all-to-all-start = ((bf16[16,768,48]{1,2,0:T(8,128)(2,1)}), bf16[16,768,48]{1,2,0:T(8,128)(2,1)S(1)}, u32[]{:S(2)}, u32[]{:S(2)}) async-start(bf16[16,768,48]{1,2,0:T(8,128)(2,1)} %broadcast_in_dim.16), calls=%async_computation | async-start | bytes 2359296 | tf_op jit(solution)/shard_map/all_to_all | solution.py:34
  30.0 0.5 copy-start.8
  93.1 1.0 copy-start.2
  96.0 1.0 copy-start.3
  96.0 2.1 copy-start.9
  96.0 7.8 %copy-start.7 = (s32[32,2]{0,1:T(2,128)S(1)}, s32[32,2]{0,1:T(2,128)}, u32[]{:S(2)}) copy-start(s32[32,2]{0,1:T(2,128)} %param.22) | copy-start | bytes 772
  96.0 29.7 %copy-start.6 = (s32[32,15]{0,1:T(8,128)S(1)}, s32[32,15]{0,1:T(8,128)}, u32[]{:S(2)}) copy-start(s32[32,15]{0,1:T(8,128)} %param.21) | copy-start | bytes 5764
  96.0 62.8 %copy-start.4 = (bf16[32,768]{1,0:T(8,128)(2,1)S(1)}, bf16[32,768]{1,0:T(8,128)(2,1)}, u32[]{:S(2)}) copy-start(bf16[32,768]{1,0:T(8,128)(2,1)} %param.23) | copy-start | bytes 147460
  99.0 11.2 %all-to-all-start.1 = ((bf16[16,2,769]{2,1,0:T(2,128)(2,1)}), bf16[16,2,769]{2,1,0:T(2,128)(2,1)S(1)}, u32[]{:S(2)}, u32[]{:S(2)}) async-start(bf16[16,2,769]{2,1,0:T(2,128)(2,1)} %pad_maximum_fusion.1), calls=%async_computation.1 | async-start | bytes 114688 | tf_op jit(solution)/shard_map/all_to_all | solution.py:46
  111.2 30.7 %all-to-all-start.2 = ((bf16[32,2,768]{2,1,0:T(2,128)(2,1)}), bf16[32,2,768]{2,1,0:T(2,128)(2,1)S(1)}, u32[]{:S(2)}, u32[]{:S(2)}) async-start(bf16[32,2,768]{2,1,0:T(2,128)(2,1)} %reshape.97), calls=%async_computation.2 | async-start | bytes 196608 | tf_op jit(solution)/shard_map/all_to_all | solution.py:179
  162.2 22.6 %all-to-all-start.4 = ((bf16[32,2,768]{2,1,0:T(2,128)(2,1)}), bf16[32,2,768]{2,1,0:T(2,128)(2,1)S(1)}, u32[]{:S(2)}, u32[]{:S(2)}) async-start(bf16[32,2,768]{2,1,0:T(2,128)(2,1)} %reshape.101), calls=%async_computation.4 | async-start | bytes 196608 | tf_op jit(solution)/shard_map/all_to_all | solution.py:189
  184.8 19.2 %all-to-all-start.3 = ((bf16[32,2,768]{2,1,0:T(2,128)(2,1)}), bf16[32,2,768]{2,1,0:T(2,128)(2,1)S(1)}, u32[]{:S(2)}, u32[]{:S(2)}) async-start(bf16[32,2,768]{2,1,0:T(2,128)(2,1)} %reshape.99), calls=%async_computation.3 | async-start | bytes 196608 | tf_op jit(solution)/shard_map/all_to_all | solution.py:179
  204.0 19.6 %all-to-all-start.5 = ((bf16[32,2,768]{2,1,0:T(2,128)(2,1)}), bf16[32,2,768]{2,1,0:T(2,128)(2,1)S(1)}, u32[]{:S(2)}, u32[]{:S(2)}) async-start(bf16[32,2,768]{2,1,0:T(2,128)(2,1)} %reshape.103), calls=%async_computation.5 | async-start | bytes 196608 | tf_op jit(solution)/shard_map/all_to_all | solution.py:189
  224.6 12.5 %all-to-all-start.6 = ((bf16[16,2,768]{2,1,0:T(2,128)(2,1)}), bf16[16,2,768]{2,1,0:T(2,128)(2,1)S(1)}, u32[]{:S(2)}, u32[]{:S(2)}) async-start(bf16[16,2,768]{2,1,0:T(2,128)(2,1)} %reshape.105), calls=%async_computation.6 | async-start | bytes 98304 | tf_op jit(solution)/shard_map/all_to_all | solution.py:221
Sparse Core Ops, SparseCore 0:
  21.7 57.3 all-gather.2
  81.1 77.5 all-gather.4
where the time goes:
time: 247 us; the launch traced here: 245 us
  waiting for transfers between devices  123 us (50%)
  starting transfers between devices  49 us (20%)
  matrix products  24.4 us (10%)
  local copies, waits for them, and re-layouts  15.5 us (6%)
  between operations  14.4 us (6%)
  blocking collectives  14.3 us (6%)
  other arithmetic  4.25 us (2%)
    all_gather x1, waiting for transfers between devices, whole_of(): nearer = lax.all_gather(x, axes[-1], axis=dim, tiled=True)  46.1 us
    all_to_all x2, waiting for transfers between devices, trade(): lax.all_to_all(leaving.reshape(graph_count, slot_count, width), 'graph',...  26.5 us
    all_to_all x2, waiting for transfers between devices, give_back(): lax.all_to_all(halo_grad.reshape(graph_count, slot_count, width), 'graph'...  23 us
    all_to_all x2, starting transfers between devices, trade(): lax.all_to_all(leaving.reshape(graph_count, slot_count, width), 'graph',...  19.4 us
    all_gather x1, waiting for transfers between devices, sent_together_2(): lax.all_gather(both, axis, axis=dim, tiled=True)  16.8 us
    all_gather x1, blocking collectives, whole_of(): nearer = lax.all_gather(x, axes[-1], axis=dim, tiled=True)  14.3 us
    all_to_all x2, starting transfers between devices, give_back(): lax.all_to_all(halo_grad.reshape(graph_count, slot_count, width), 'graph'...  13.4 us
    all_to_all x1, waiting for transfers between devices, sent_together(): lax.all_to_all(both, axis, split_axis=split_dim, concat_axis=concat_dim,...  6.28 us
  transfers between devices with their start and end apart: 9, of which 8 were waited for; matrix products, arithmetic and copies ran while one was open for 16% of the time, Pallas kernels for 0%

commit v1 on v0

v1 whole, which is shorter than its diff:
```python
import functools

import jax
import jax.numpy as jnp
from jax import lax
from jax.experimental import pallas as pl
from jax.experimental.pallas import tpu as pltpu
from jax.sharding import PartitionSpec as P

D = 768
HEAD = 64
HEADS = 12
BLOCK = 128
BLOCKS = 4
ROWS = 32
FAN = 15
N_TEXT = 16
N_GRAPH = 32
RING = 16
PIECE = 48
TILE = 16
CHUNKS = D // 128
EPS = 1e-06
MESH = pl.DeviceIdType.MESH
f32 = jnp.float32
bf16 = jnp.bfloat16


def mm(a, b):
    return lax.dot_general(a, b, (((1,), (0,)), ((), ())), preferred_element_type=f32)


def mm_t(a, b):
    return lax.dot_general(a, b, (((1,), (1,)), ((), ())), preferred_element_type=f32)


def iota(shape, dim):
    return lax.broadcasted_iota(jnp.int32, shape, dim)


def one_hot(condition):
    return jnp.where(condition, 1.0, 0.0).astype(bf16)


def eye(n):
    return one_hot(iota((n, n), 0) == iota((n, n), 1))


def transposed(x):
    return mm_t(eye(x.shape[1]), x).astype(bf16)


def stacked(x):
    return jnp.concatenate([x[:, j * 128 : (j + 1) * 128] for j in range(CHUNKS)], axis=0)


def unstacked(x):
    rows = x.shape[0] // CHUNKS
    return jnp.concatenate([x[j * rows : (j + 1) * rows] for j in range(CHUNKS)], axis=1)


def aligned(x):
    return pl.multiple_of(x, 16)


def kernel(
    tokens,
    attn_qkv,
    attn_out,
    sage_one,
    sage_two,
    out_grad,
    doc_ids,
    in_gain,
    in_bias,
    owner_text,
    neighbours,
    boundary,
    node_states,
    abstract_grad,
    tok,
    qkv_own,
    out_own,
    grad_in,
    wt,
    sage,
    normed,
    qk,
    pooled,
    mix,
    member,
    pj,
    pjt,
    aj,
    ajt,
    sj,
    sjt,
    flag_out,
    flag_in,
    emb_out,
    emb_in,
    one_out,
    one_in,
    two_out,
    two_in,
    back_two_out,
    back_two_in,
    back_one_out,
    back_one_in,
    ret_out,
    ret_in,
    load_sem,
    wt_sem,
    wt_send,
    wt_pair_send,
    z_sem,
    z_send,
    pair_sem,
    pair_send,
    ex_send,
    ex_recv,
):
    t = lax.axis_index("text")
    g = lax.axis_index("graph")
    y, x = t // 4, t % 4
    z, c = g // 2, g % 2
    sibling = (t, z * 2 + 1 - c)

    barrier = pltpu.get_barrier_semaphore()

    def greet_text(i, carry):
        pl.semaphore_signal(barrier, inc=1, device_id=((t + i) % N_TEXT, g), device_id_type=MESH)
        return carry

    def greet_graph(i, carry):
        pl.semaphore_signal(barrier, inc=1, device_id=(t, (g + i) % N_GRAPH), device_id_type=MESH)
        return carry

    lax.fori_loop(1, N_TEXT, greet_text, 0)
    lax.fori_loop(1, N_GRAPH, greet_graph, 0)

    own_rows = pl.ds(aligned(g * PIECE), PIECE)
    loads = [
        pltpu.make_async_copy(attn_qkv, qkv_own, load_sem.at[0]),
        pltpu.make_async_copy(attn_out, out_own, load_sem.at[1]),
        pltpu.make_async_copy(sage_one, sage.at[0, own_rows], load_sem.at[2]),
        pltpu.make_async_copy(sage_two, sage.at[1, own_rows], load_sem.at[3]),
        pltpu.make_async_copy(tokens, tok, load_sem.at[4]),
        pltpu.make_async_copy(out_grad, grad_in, load_sem.at[5]),
    ]
    for load in loads:
        load.start()
    loads[0].wait()
    wt[pl.ds(aligned(t * 144), 144), :] = mm_t(eye(144), qkv_own[...]).astype(bf16)
    loads[1].wait()
    wt[pl.ds(aligned(2304 + t * PIECE), PIECE), :] = mm_t(eye(48), out_own[...]).astype(bf16)
    loads[2].wait()
    loads[3].wait()
    pl.semaphore_wait(barrier, N_TEXT + N_GRAPH - 2)

    def sage_rows(zz):
        return pl.ds(aligned((zz * 2 + c) * PIECE), PIECE)

    def sage_send(ref, way, step, rows_of):
        forward = (z + 1 + RING - 2 * way) % RING
        pltpu.make_async_remote_copy(
            ref, ref, z_send, z_sem.at[way, step], device_id=(t, forward * 2 + c), device_id_type=MESH
        ).start()

    def sage_pair(ref):
        pltpu.make_async_remote_copy(
            ref, ref, pair_send, pair_sem, device_id=sibling, device_id_type=MESH
        ).start()

    def arrived(ref, sem):
        pltpu.make_async_copy(ref, ref, sem).wait()

    def sage_step(step, last=False):
        for way in (0, 1):
            source = (z + RING - step) % RING if way == 0 else (z + step) % RING
            ref = sage.at[:, sage_rows(source)]
            arrived(ref, z_sem.at[way, step])
            sage_send(sage.at[way, sage_rows(source)] if last else ref, way, step + 1, None)
            sage_pair(ref)

    def sage_end():
        for way in (0, 1):
            ref = sage.at[way, sage_rows((z + 8) % RING)]
            arrived(ref, z_sem.at[way, 8])
            sage_pair(ref)

    def chip(first, second):
        a, b = (first + 4) % 4, (second + 4) % 4
        return (1 - c) * (b * 4 + a) + c * (a * 4 + b)

    pa = (1 - c) * x + c * y
    pb = (1 - c) * y + c * x

    def piece_row(owner, i, core):
        if i == 0:
            return owner * 144 + core * PIECE
        other = (core + owner) % 2
        return (1 - other) * (owner * 144 + 96) + other * (2304 + owner * PIECE)

    def wt_ref(row):
        return wt.at[pl.ds(aligned(row), PIECE)]

    def wt_push(row, to, send=None):
        pltpu.make_async_remote_copy(
            wt_ref(row),
            wt_ref(row),
            wt_send,
            wt_sem.at[row // PIECE],
            device_id=(to, g),
            device_id_type=MESH,
        ).start()

    def wt_pair(row):
        pltpu.make_async_remote_copy(
            wt_ref(row),
            wt_ref(row),
            wt_pair_send,
            wt_sem.at[row // PIECE],
            device_id=sibling,
            device_id_type=MESH,
        ).start()

    a_plus, a_minus = chip(pa + 1, pb), chip(pa - 1, pb)
    b_plus, b_minus = chip(pa, pb + 1), chip(pa, pb - 1)

    for i in (0, 1):
        row = piece_row(t, i, c)
        for to in (a_plus, a_minus, b_plus, b_minus):
            wt_push(row, to)
    own = sage.at[:, sage_rows(z)]
    sage_send(own, 0, 1, None)
    sage_send(own, 1, 1, None)
    sage_pair(own)

    def wt_take(da, db, i, targets):
        row = piece_row(chip(pa + da, pb + db), i, c)
        arrived(wt_ref(row), wt_sem.at[row // PIECE])
        for to in targets:
            wt_push(row, to)
        wt_pair(row)

    loads[4].wait()

    def norm_block(b, carry):
        rows = pl.ds(aligned(b * BLOCK), BLOCK)
        states = tok[rows, :].astype(f32)
        mean = jnp.mean(states, axis=1, keepdims=True)
        centred = states - mean
        variance = jnp.mean(centred * centred, axis=1, keepdims=True)
        normed[rows, :] = (
            centred * lax.rsqrt(variance + EPS) * in_gain[...] + in_bias[...]
        ).astype(bf16)
        return carry

    lax.fori_loop(0, BLOCKS, norm_block, 0)

    wt_take(-1, 0, 0, (b_plus, b_minus, a_plus))
    wt_take(1, 0, 0, (b_plus, b_minus))
    wt_take(0, -1, 0, (b_plus,))
    wt_take(0, 1, 0, ())
    wt_take(-1, 0, 1, (b_plus, b_minus))
    wt_take(1, 0, 1, (b_plus, b_minus, a_minus))
    wt_take(0, -1, 1, ())
    wt_take(0, 1, 1, (b_minus,))
    sage_step(1)

    def exchange(src, dst, k, me, count, peer):
        def send(i, carry):
            to = (me + i) % count
            pltpu.make_async_remote_copy(
                src.at[pl.ds(aligned(to * TILE), TILE)],
                dst.at[pl.ds(aligned(me * TILE), TILE)],
                ex_send.at[k],
                ex_recv.at[k],
                device_id=peer(to),
                device_id_type=MESH,
            ).start()
            return carry

        lax.fori_loop(1, count, send, 0)
        mine = pl.ds(aligned(me * TILE), TILE)
        dst[mine, :] = src[mine, :]

    def over_text(src, dst, k):
        exchange(src, dst, k, t, N_TEXT, lambda to: (to, g))

    def over_graph(src, dst, k):
        exchange(src, dst, k, g, N_GRAPH, lambda to: (t, to))

    def finish(ref, sem, k, count):
        part = ref.at[pl.ds(0, (count - 1) * TILE)]
        pltpu.make_async_copy(part, part, sem.at[k]).wait()

    owner = owner_text[...].astype(f32)
    lane_abstract = iota((16, 96), 1) % 16
    sub_abstract = iota((16, 96), 0)
    target = jnp.sum(jnp.where(lane_abstract == sub_abstract, owner, 0.0), axis=0, keepdims=True)
    earlier = jnp.sum(
        jnp.where((sub_abstract < lane_abstract) & (owner == target), 1.0, 0.0),
        axis=0,
        keepdims=True,
    )
    slot = target * 2.0 + earlier
    r = iota((256, 96), 0)
    lane = iota((256, 96), 1)
    place = r % 16
    cap = jnp.where(place >= 6, 1, 0)
    slot_row = ((r // 16) * 2 + cap).astype(f32)
    sj[...] = one_hot((place < 12) & (place - 6 * cap == lane // 16) & (slot_row == slot))
    flags = one_hot(
        (place < 2) & (lane < 16) & (((r // 16) * 2 + place).astype(f32) == slot)
    )
    flag_out[...] = mm(flags, jnp.ones((96, 128), bf16)).astype(bf16)
    over_text(flag_out, flag_in, 0)
    sjt[...] = transposed(sj[...])

    wt_take(2, 0, 0, (b_plus, b_minus))
    wt_take(2, 0, 1, (b_plus, b_minus))
    wt_take(-1, -1, 0, (b_plus,))
    wt_take(-1, 1, 0, ())
    wt_take(1, -1, 0, (b_plus,))
    wt_take(1, 1, 0, ())

    r = iota((512, 192), 0)
    place = r % 16
    second = jnp.where(place >= 6, 1, 0)
    same_chunk = (place < 12) & (place - 6 * second == iota((512, 192), 1) // 32)
    tile_of = one_hot(iota((32, 192), 0) == iota((32, 192), 1) % 32)
    nbr = mm(
        mm_t(eye(FAN), neighbours[...].astype(f32).astype(bf16)).astype(bf16), tile_of
    )
    listed = iota((96, 192), 0).astype(f32)
    adj_t = jnp.zeros((96, 192), f32)
    for k in range(FAN):
        adj_t = adj_t + jnp.where(listed == nbr[k : k + 1, :], 1.0, 0.0)
    adj_t = adj_t.astype(bf16)
    r64 = iota((512, 64), 0)
    place64 = r64 % 16
    halo_of = one_hot(
        (place64 < 12)
        & ((r64 // 16) * 2 + jnp.where(place64 >= 6, 1, 0) == iota((512, 64), 1))
    )
    aj[...] = jnp.where(same_chunk, mm(halo_of, adj_t[32:96, :]), 0.0).astype(bf16)
    ajt[...] = transposed(aj[...])
    own_adj_t = adj_t[0:32, 0:32]
    own_adj = transposed(own_adj_t)
    node_lane = iota((32, 192), 1) % 32
    bnd = boundary[...]
    r32 = iota((512, 32), 0)
    place32 = r32 % 16
    peer32 = r32 // 16 == iota((512, 32), 1)
    picked = mm(one_hot(peer32 & (place32 < 6)), one_hot(bnd[:, 0:1] == node_lane)) + mm(
        one_hot(peer32 & (place32 >= 6) & (place32 < 12)), one_hot(bnd[:, 1:2] == node_lane)
    )
    pj[...] = jnp.where(same_chunk, picked, 0.0).astype(bf16)
    pjt[...] = transposed(pj[...])
    n = iota((192, 256), 0)
    m = iota((192, 256), 1)
    uj = one_hot((m // 16 == (n % 32) // 2) & (m % 16 == (n % 2) * 6 + n // 32))
    m = iota((256, 192), 0)
    n = iota((256, 192), 1)
    ujt = one_hot((m // 16 == (n % 32) // 2) & (m % 16 == (n % 2) * 6 + n // 32))

    wt_take(-1, -1, 1, ())
    wt_take(-1, 1, 1, (b_minus,))
    wt_take(1, -1, 1, ())
    wt_take(1, 1, 1, (b_minus,))
    sage_step(2)
    wt_take(2, -1, 0, (b_plus,))
    wt_take(2, 1, 0, ())
    wt_take(2, -1, 1, ())
    wt_take(2, 1, 1, (b_minus,))
    wt_take(0, 2, 0, ())
    wt_take(0, 2, 1, ())
    wt_take(-1, 2, 0, ())
    wt_take(-1, 2, 1, ())
    wt_take(1, 2, 0, ())
    wt_take(1, 2, 1, ())
    sage_step(3)
    wt_take(2, 2, 0, ())
    wt_take(2, 2, 1, ())

    def wait_pair(early):
        def one(tt, carry):
            for i in (0, 1):
                row = piece_row(tt, i, 1 - c)
                wanted = row < 1536 if early else row >= 1536

                @pl.when((tt != t) & wanted)
                def _():
                    arrived(wt_ref(row), wt_sem.at[row // PIECE])

            return carry

        lax.fori_loop(0, N_TEXT, one, 0)

    wait_pair(True)

    def project(k, carry):
        cols = pl.ds(pl.multiple_of(k * 256, 256), 256)
        qk[:, cols] = mm_t(normed[...], wt[cols, :]).astype(bf16)
        return carry

    lax.fori_loop(0, 6, project, 0)

    ones = jnp.ones((BLOCK, BLOCK), bf16)
    low = iota((BLOCK, BLOCK), 1) < HEAD
    mix[...] = jnp.where(iota((16, BLOCK), 0) == HEADS, 1.0, 0.0)

    def attend(b, carry):
        rows = pl.ds(aligned(b * BLOCK), BLOCK)
        docs = doc_ids[pl.ds(b, 1), :]
        docs_here = jnp.broadcast_to(docs, (BLOCK, BLOCK)).astype(f32)
        docs_there = mm_t(eye(BLOCK), docs_here.astype(bf16))
        same = docs_here == docs_there
        same = jnp.concatenate([same, same], axis=0)
        for pair in range(HEADS // 2):
            lanes = slice(pair * 128, (pair + 1) * 128)
            q = qk[rows, lanes]
            key = qk[rows, D + pair * 128 : D + (pair + 1) * 128]
            zero = jnp.zeros_like(q)
            both = jnp.concatenate([jnp.where(low, q, zero), jnp.where(low, zero, q)], axis=0)
            scores = mm_t(both, key) * HEAD ** (-0.5)
            weights = jnp.where(same, jnp.exp(scores), 0.0)
            sums = mm(weights.astype(bf16), ones)
            probs = weights / sums
            mix[2 * pair : 2 * pair + 1, :] = jnp.sum(probs[:BLOCK], axis=0, keepdims=True)
            mix[2 * pair + 1 : 2 * pair + 2, :] = jnp.sum(probs[BLOCK:], axis=0, keepdims=True)
        heads = mix[...]
        doc_f = docs.astype(f32)
        spread = jnp.concatenate(
            [heads * jnp.where(doc_f == float(j), 1.0, 0.0) for j in range(4)], axis=0
        )
        pooled[pl.ds(aligned(b * 64), 64), :] = mm(spread.astype(bf16), normed[rows, :])
        sage_step(b + 4, False) if False else None
        return carry

    attend(0, 0)
    sage_step(4)
    attend(1, 0)
    sage_step(5)
    attend(2, 0)
    sage_step(6)
    attend(3, 0)
    sage_step(7, True)

    wait_pair(False)
    sums = pooled[...]
    high = sums.astype(bf16)
    rest = (sums - high.astype(f32)).astype(bf16)
    per_head = mm_t(high, wt[1536:2304, :])
    chosen = iota((256, D), 0) % 16 == iota((256, D), 1) // HEAD
    doc_of = iota((16, 256), 0) == iota((16, 256), 1) // 16
    context = mm(one_hot(doc_of), jnp.where(chosen, per_head, 0.0).astype(bf16)).astype(bf16)
    plain = one_hot(doc_of & (iota((16, 256), 1) % 16 == HEADS))
    pooled_norm = mm(plain, high) + mm(plain, rest)
    doc_row = iota((16, BLOCK), 0)
    docs = doc_ids[...]
    docs16 = jnp.where(
        doc_row < 8,
        jnp.where(doc_row < 4, docs[0:1, :], docs[1:2, :]),
        jnp.where(doc_row < 12, docs[2:3, :], docs[3:4, :]),
    )
    lengths = jnp.sum(jnp.where(docs16 == doc_row % 4, 1.0, 0.0), axis=1, keepdims=True)
    total = pooled_norm + mm_t(context, wt[2304:3072, :])
    embedded = (total / lengths).astype(bf16)
    emb_out[...] = mm(sj[...], stacked(embedded)).astype(bf16)
    over_text(emb_out, emb_in, 1)

    sage_end()
    whole = sage.at[:, pl.ds(0, 768)]
    pltpu.make_async_copy(whole, whole, pair_sem).wait()
    finish(flag_in, ex_recv, 0, N_TEXT)
    live = mm(
        one_hot(
            (iota((32, 256), 1) // 16 == iota((32, 256), 0) // 2)
            & (iota((32, 256), 1) % 16 == iota((32, 256), 0) % 2)
        ),
        flag_in[...],
    )[:, 0:1]
    loads[5].wait()

    def spread_of(u, layer):
        return (mm_t(u, sage[layer, D : 2 * D, :]) / FAN).astype(bf16)

    def send_back(spread, dst_out, dst_in, k):
        dst_out[...] = mm(aj[...], stacked(spread)).astype(bf16)
        over_graph(dst_out, dst_in, k)

    grad_two = (live * grad_in[...].astype(f32)).astype(bf16)
    spread_two = spread_of(grad_two, 1)
    send_back(spread_two, back_two_out, back_two_in, 2)
    finish(emb_in, ex_recv, 1, N_TEXT)
    v_stack = mm(uj, emb_in[...]).astype(bf16)
    one_out[...] = mm(pj[...], v_stack).astype(bf16)
    over_graph(one_out, one_in, 3)
    v = unstacked(v_stack)
    into_one = mm_t(grad_two, sage[1, 0:D, :]) + mm(own_adj_t, spread_two)
    preact = mm(v, sage[0, 0:D, :])
    own_part = mm(own_adj, v)
    finish(back_two_in, ex_recv, 2, N_GRAPH)
    into_one = into_one + unstacked(mm(pjt[...], back_two_in[...]))

    finish(one_in, ex_recv, 3, N_GRAPH)
    aggregated = ((own_part + unstacked(mm(ajt[...], one_in[...]))) / FAN).astype(bf16)
    preact = preact + mm(aggregated, sage[0, D : 2 * D, :])
    slope = 0.7978845608028654
    squared = preact * preact
    bent = jnp.tanh(slope * (preact + 0.044715 * squared * preact))
    hidden = (live * (0.5 * preact * (1.0 + bent))).astype(bf16)
    steep = 0.5 * (1.0 + bent) + 0.5 * preact * (1.0 - bent * bent) * (
        slope * (1.0 + 3.0 * 0.044715 * squared)
    )
    grad_one = (live * steep * into_one).astype(bf16)
    spread_one = spread_of(grad_one, 0)
    send_back(spread_one, back_one_out, back_one_in, 4)
    two_out[...] = mm(pj[...], stacked(hidden)).astype(bf16)
    over_graph(two_out, two_in, 5)
    embed_grad = mm_t(grad_one, sage[0, 0:D, :]) + mm(own_adj_t, spread_one)
    preact_two = mm(hidden, sage[1, 0:D, :])
    own_two = mm(own_adj, hidden)

    finish(back_one_in, ex_recv, 4, N_GRAPH)
    embed_grad = (embed_grad + unstacked(mm(pjt[...], back_one_in[...]))).astype(bf16)
    ret_out[...] = mm(ujt, stacked(embed_grad)).astype(bf16)
    over_text(ret_out, ret_in, 6)

    finish(two_in, ex_recv, 5, N_GRAPH)
    aggregated = ((own_two + unstacked(mm(ajt[...], two_in[...]))) / FAN).astype(bf16)
    preact_two = preact_two + mm(aggregated, sage[1, D : 2 * D, :])
    node_states[...] = (live * preact_two).astype(bf16)

    finish(ret_in, ex_recv, 6, N_TEXT)
    abstract_grad[...] = unstacked(mm(sjt[...], ret_in[...]).astype(bf16))

    arrived(wt.at[pl.ds(0, 30 * PIECE)], wt_send)
    arrived(wt.at[pl.ds(0, 30 * PIECE)], wt_pair_send)
    arrived(sage.at[0, pl.ds(0, 30 * PIECE)], z_send)
    arrived(sage.at[:, pl.ds(0, 768)], pair_send)
    for k, (ref, count) in enumerate(
        (
            (flag_out, N_TEXT),
            (emb_out, N_TEXT),
            (back_two_out, N_GRAPH),
            (one_out, N_GRAPH),
            (back_one_out, N_GRAPH),
            (two_out, N_GRAPH),
            (ret_out, N_TEXT),
        )
    ):
        finish(ref, ex_send, k, count)


def local(
    tokens,
    doc_ids,
    in_gain,
    in_bias,
    attn_qkv,
    attn_out,
    owner_text,
    sage_one,
    sage_two,
    neighbours,
    boundary,
    out_grad,
):
    anywhere = pl.BlockSpec(memory_space=pl.ANY)
    vmem = pl.BlockSpec(memory_space=pltpu.VMEM)
    text_tiles = pltpu.VMEM((N_TEXT * TILE, 128), bf16)
    graph_tiles = pltpu.VMEM((N_GRAPH * TILE, 128), bf16)
    return pl.pallas_call(
        kernel,
        out_shape=(
            jax.ShapeDtypeStruct((ROWS, D), bf16),
            jax.ShapeDtypeStruct((16, D), bf16),
        ),
        in_specs=[anywhere] * 6 + [vmem] * 6,
        out_specs=(vmem, vmem),
        scratch_shapes=[
            pltpu.VMEM((512, D), bf16),
            pltpu.VMEM((D, 144), bf16),
            pltpu.VMEM((D, 48), bf16),
            pltpu.VMEM((ROWS, D), bf16),
            pltpu.VMEM((3072, D), bf16),
            pltpu.VMEM((2, 2 * D, D), bf16),
            pltpu.VMEM((512, D), bf16),
            pltpu.VMEM((512, 2 * D), bf16),
            pltpu.VMEM((256, D), f32),
            pltpu.VMEM((16, BLOCK), f32),
            pltpu.VMEM((16, BLOCK), f32),
            pltpu.VMEM((512, 192), bf16),
            pltpu.VMEM((192, 512), bf16),
            pltpu.VMEM((512, 192), bf16),
            pltpu.VMEM((192, 512), bf16),
            pltpu.VMEM((256, 96), bf16),
            pltpu.VMEM((96, 256), bf16),
            text_tiles,
            text_tiles,
            text_tiles,
            text_tiles,
            graph_tiles,
            graph_tiles,
            graph_tiles,
            graph_tiles,
            graph_tiles,
            graph_tiles,
            graph_tiles,
            graph_tiles,
            text_tiles,
            text_tiles,
            pltpu.SemaphoreType.DMA((6,)),
            pltpu.SemaphoreType.DMA((64,)),
            pltpu.SemaphoreType.DMA,
            pltpu.SemaphoreType.DMA,
            pltpu.SemaphoreType.DMA((2, 9)),
            pltpu.SemaphoreType.DMA,
            pltpu.SemaphoreType.DMA,
            pltpu.SemaphoreType.DMA,
            pltpu.SemaphoreType.DMA((7,)),
            pltpu.SemaphoreType.DMA((7,)),
        ],
        compiler_params=pltpu.CompilerParams(
            collective_id=0, has_side_effects=True, vmem_limit_bytes=48 * 1024 * 1024
        ),
    )(
        tokens,
        attn_qkv,
        attn_out,
        sage_one,
        sage_two,
        out_grad,
        doc_ids,
        in_gain.reshape(1, D),
        in_bias.reshape(1, D),
        owner_text,
        neighbours,
        boundary,
    )


def solution(mesh):
    split = P(("text", "graph"), None)
    return jax.shard_map(
        local,
        mesh=mesh,
        in_specs=(
            split,
            split,
            P(None),
            P(None),
            P(None, "text"),
            P(None, "text"),
            split,
            P("graph", None),
            P("graph", None),
            split,
            split,
            split,
        ),
        out_specs=(split, split),
        check_vma=False,
    )
```

time: 247 us -> 106 us (0.43)
  waiting for transfers between devices: 123 us -> 0 us
  Pallas kernels: 0 us -> 97.9 us
  starting transfers between devices: 49 us -> 0 us
  matrix products: 24.4 us -> 0 us
  blocking collectives: 14.3 us -> 0 us
  between operations: 14.4 us -> 0.73 us
  local copies, waits for them, and re-layouts: 15.5 us -> 7.29 us
  other arithmetic: 4.25 us -> 0 us
    pallas_call x0 -> x1, Pallas kernels: none -> 97.9 us  [local(): pl.pallas_call(kernel, out_shape=(jax.ShapeDtypeStruct((ROWS, D), bf16),...]
    all_gather x2 -> x0, waiting for transfers between devices: 62.9 us -> none  [the longest x1 46.1 us: whole_of(): nearer = lax.all_gather(x, axes[-1], axis=dim, tiled=True)]
    all_to_all x7 -> x0, waiting for transfers between devices: 60 us -> none  [the longest x2 26.5 us: trade(): lax.all_to_all(leaving.reshape(graph_count, slot_count, width), 'graph',...]
    all_to_all x7 -> x0, starting transfers between devices: 48.9 us -> none  [the longest x2 19.4 us: trade(): lax.all_to_all(leaving.reshape(graph_count, slot_count, width), 'graph',...]
    dot_general x19 -> x0, matrix products: 24.4 us -> none  [the longest x1 5.62 us: local(): jnp.dot(normed, whole_of(attn_qkv, TEXT, 1), preferred_element_type=jnp.f...]
    all_gather x1 -> x0, blocking collectives: 14.3 us -> none  [whole_of(): nearer = lax.all_gather(x, axes[-1], axis=dim, tiled=True)]
    reshape x13 -> x2, local copies, waits for them, and re-layouts: 7.78 us -> 0.77 us  [the longest x1 0.76 us: local(): in_gain.reshape(1, D)]
    unnamed x27 -> x19, local copies, waits for them, and re-layouts: 0.25 us -> 6.52 us
  transfers between devices with their start and end apart: 9 -> 0, of which waited for: 8 -> 0; matrix products, arithmetic and copies ran while one was open for 16% -> 0% of each run, Pallas kernels for 0% -> 0%
where the time goes in v1:
time: 106 us
  Pallas kernels  97.9 us (92%)
  local copies, waits for them, and re-layouts  7.29 us (7%)
    pallas_call x1, Pallas kernels, local(): pl.pallas_call(kernel, out_shape=(jax.ShapeDtypeStruct((ROWS, D), bf16),...  97.9 us
    unnamed x19, local copies, waits for them, and re-layouts  6.52 us

profile of v1, /device:TPU:1, one launch (start us, length us, event | category | flops | bytes accessed | tf_op | source)
XLA Modules:
  0.0 105.9 jit_solution(16774894996996206838)
XLA Ops:
  0.6 0.0 copy-start.5
  0.6 0.0 copy-start
  0.6 0.8 reshape.10.in_gain
  1.4 0.0 copy-done.5
  1.4 0.7 copy.16.owner_text
  2.2 0.8 copy.17.neighbours
  2.9 0.8 copy.18.boundary
  3.7 1.0 copy.15.attn_out
  4.7 0.0 copy-start.1
  4.8 0.0 copy-start.2
  4.8 0.0 copy-start.4
  4.8 1.2 %copy.14.attn_qkv = bf16[768,144]{1,0:T(8,128)(2,1)S(1)} copy(bf16[768,144]{0,1:T(8,128)(2,1)} %param.16) | data formatting | bytes 442368 | tf_op args[4]
  5.9 0.0 copy-done
  6.0 0.0 copy-done.1
  6.0 0.0 copy-done.2
  6.0 0.0 copy-done.4
  6.0 0.0 copy-start.3
  6.0 0.8 copy-done.3
  6.8 97.9 %shard_map.131 = (bf16[32,768]{1,0:T(8,128)(2,1)S(1)}, bf16[16,768]{1,0:T(8,128)(2,1)S(1)}) custom-call(bf16[512,768]{1,0:T(8,128)(2,1)S(1)} %copy-done, bf16[768,144]{1,0:T(8,128)(2,1)S(1)} %copy.14.attn_qkv, bf16[768,48]{1,0:T(8,128)(2,1)S(1)} %copy.15.attn_out, bf16[48,768]{1,0:T(8,128)(2,1)S(1)} %copy-done.1, bf16[48,768]{1,0:T(8,128)(2,1)S(1)} %copy-done.2, ...), custom_call_target="tpu_custom_call" | custom-call | tf_op jit(solution)/shard_map/pallas_call | solution.py:577
  104.7 0.6 copy.21
  105.3 0.6 copy.22
  (1 shorter events, 0.0 us)
Async XLA Ops:
  0.6 0.8 copy-start.5
  0.6 5.3 %copy-start = (bf16[512,768]{1,0:T(8,128)(2,1)S(1)}, bf16[512,768]{1,0:T(8,128)(2,1)}, u32[]{:S(2)}) copy-start(bf16[512,768]{1,0:T(8,128)(2,1)} %tokens.1) | copy-start | bytes 2359300
  4.7 1.2 %copy-start.1 = (bf16[48,768]{1,0:T(8,128)(2,1)S(1)}, bf16[48,768]{1,0:T(8,128)(2,1)}, u32[]{:S(2)}) copy-start(bf16[48,768]{1,0:T(8,128)(2,1)} %sage_one.1) | copy-start | bytes 221188
  4.8 1.2 %copy-start.2 = (bf16[48,768]{1,0:T(8,128)(2,1)S(1)}, bf16[48,768]{1,0:T(8,128)(2,1)}, u32[]{:S(2)}) copy-start(bf16[48,768]{1,0:T(8,128)(2,1)} %sage_two.1) | copy-start | bytes 221188
  4.8 1.2 %copy-start.4 = (s32[4,128]{1,0:T(4,128)S(1)}, s32[4,128]{1,0:T(4,128)}, u32[]{:S(2)}) copy-start(s32[4,128]{1,0:T(4,128)} %doc_ids.1) | copy-start | bytes 6148
  6.0 0.8 copy-start.3

commit v2 on v1

v2 whole, which is shorter than its diff:
```python
import functools

import jax
import jax.numpy as jnp
from jax import lax
from jax.experimental import pallas as pl
from jax.experimental.pallas import tpu as pltpu
from jax.sharding import PartitionSpec as P

D = 768
HEAD = 64
HEADS = 12
BLOCK = 128
BLOCKS = 4
ROWS = 32
FAN = 15
N_TEXT = 16
N_GRAPH = 32
RING = 16
PIECE = 48
TILE = 16
CHUNKS = D // 128
EPS = 1e-06
FAR_FIRST = sorted(
    [(dy, dx) for dy in range(4) for dx in range(4) if dy or dx],
    key=lambda d: (min(d[0], 4 - d[0]) + min(d[1], 4 - d[1]), d),
    reverse=True,
)
MESH = pl.DeviceIdType.MESH
f32 = jnp.float32
bf16 = jnp.bfloat16


def mm(a, b):
    return lax.dot_general(a, b, (((1,), (0,)), ((), ())), preferred_element_type=f32)


def mm_t(a, b):
    return lax.dot_general(a, b, (((1,), (1,)), ((), ())), preferred_element_type=f32)


def iota(shape, dim):
    return lax.broadcasted_iota(jnp.int32, shape, dim)


def one_hot(condition):
    return jnp.where(condition, 1.0, 0.0).astype(bf16)


def eye(n):
    return one_hot(iota((n, n), 0) == iota((n, n), 1))


def transposed(x):
    return mm_t(eye(x.shape[1]), x).astype(bf16)


def stacked(x):
    return jnp.concatenate([x[:, j * 128 : (j + 1) * 128] for j in range(CHUNKS)], axis=0)


def unstacked(x):
    rows = x.shape[0] // CHUNKS
    return jnp.concatenate([x[j * rows : (j + 1) * rows] for j in range(CHUNKS)], axis=1)


def aligned(x):
    return pl.multiple_of(x, 16)


def kernel(
    tokens,
    attn_qkv,
    attn_out,
    sage_one,
    sage_two,
    out_grad,
    doc_ids,
    in_gain,
    in_bias,
    owner_text,
    neighbours,
    boundary,
    node_states,
    abstract_grad,
    tok,
    grad_in,
    wt,
    sage_own,
    sage,
    normed,
    qk,
    pooled,
    mix,
    member,
    pj,
    pjt,
    aj,
    ajt,
    sj,
    sjt,
    flag_out,
    flag_in,
    emb_out,
    emb_in,
    one_out,
    one_in,
    two_out,
    two_in,
    back_two_out,
    back_two_in,
    back_one_out,
    back_one_in,
    ret_out,
    ret_in,
    load_sem,
    wt_sem,
    wt_send,
    wt_pair_send,
    spread_send,
    spread_sem,
    unit_send,
    unit_sem,
    pair_sem,
    pair_send,
    ex_send,
    ex_recv,
):
    t = lax.axis_index("text")
    g = lax.axis_index("graph")
    y, x = t // 4, t % 4
    z, c = g // 2, g % 2
    sibling = (t, z * 2 + 1 - c)

    barrier = pltpu.get_barrier_semaphore()

    def greet_text(i, carry):
        pl.semaphore_signal(barrier, inc=1, device_id=((t + i) % N_TEXT, g), device_id_type=MESH)
        return carry

    def greet_graph(i, carry):
        pl.semaphore_signal(barrier, inc=1, device_id=(t, (g + i) % N_GRAPH), device_id_type=MESH)
        return carry

    lax.fori_loop(1, N_GRAPH, greet_graph, 0)
    lax.fori_loop(1, N_TEXT, greet_text, 0)

    own_qkv = wt.at[pl.ds(aligned(t * 144), 144)]
    own_out = wt.at[pl.ds(aligned(2304 + t * PIECE), PIECE)]
    loads = [
        pltpu.make_async_copy(attn_qkv, own_qkv, load_sem.at[0]),
        pltpu.make_async_copy(attn_out, own_out, load_sem.at[1]),
        pltpu.make_async_copy(sage_one, sage_own.at[0], load_sem.at[2]),
        pltpu.make_async_copy(sage_two, sage_own.at[1], load_sem.at[3]),
        pltpu.make_async_copy(tokens, tok, load_sem.at[4]),
        pltpu.make_async_copy(out_grad, grad_in, load_sem.at[5]),
    ]
    for load in loads:
        load.start()
    for load in loads[:4]:
        load.wait()
    pl.semaphore_wait(barrier, N_TEXT + N_GRAPH - 2)

    def arrived(ref, sem):
        pltpu.make_async_copy(ref, ref, sem).wait()

    def chip(first, second):
        a, b = (first + 4) % 4, (second + 4) % 4
        return (1 - c) * (b * 4 + a) + c * (a * 4 + b)

    pa = (1 - c) * x + c * y
    pb = (1 - c) * y + c * x

    def piece_row(owner, i, core):
        if i == 0:
            return owner * 144 + core * PIECE
        other = (core + owner) % 2
        return (1 - other) * (owner * 144 + 96) + other * (2304 + owner * PIECE)

    def wt_ref(row):
        return wt.at[pl.ds(aligned(row), PIECE)]

    def wt_push(row, to, send=None):
        pltpu.make_async_remote_copy(
            wt_ref(row),
            wt_ref(row),
            wt_send,
            wt_sem.at[row // PIECE],
            device_id=(to, g),
            device_id_type=MESH,
        ).start()

    def wt_pair(row):
        pltpu.make_async_remote_copy(
            wt_ref(row),
            wt_ref(row),
            wt_pair_send,
            wt_sem.at[row // PIECE],
            device_id=sibling,
            device_id_type=MESH,
        ).start()

    a_plus, a_minus = chip(pa + 1, pb), chip(pa - 1, pb)
    b_plus, b_minus = chip(pa, pb + 1), chip(pa, pb - 1)

    for i in (0, 1):
        row = piece_row(t, i, c)
        for to in (a_plus, a_minus, b_plus, b_minus):
            wt_push(row, to)

    def tile(layer, m, core):
        return sage.at[layer, m, pl.ds(aligned((core * 16 + t) * TILE), TILE)]

    def source_of(m, core):
        return (core * 16 + t + 32 * m) // 3

    def spread_out(layer):
        for m in range(3):
            for core in (0, 1):

                @pl.when(source_of(m, core) == g)
                def _():
                    at = aligned((core * 16 + t + 32 * m - 3 * g) * TILE)

                    def push(to):
                        pltpu.make_async_remote_copy(
                            sage_own.at[layer, pl.ds(at, TILE)],
                            tile(layer, m, core),
                            spread_send,
                            spread_sem.at[layer, m],
                            device_id=(t, to),
                            device_id_type=MESH,
                        ).start()

                    def far(i, carry):
                        push((z + i) % RING * 2 + core)
                        return carry

                    lax.fori_loop(1, RING, far, 0)

                    @pl.when(c != core)
                    def _():
                        push(z * 2 + core)

                    @pl.when(c == core)
                    def _():
                        sage[layer, m, pl.ds(aligned((core * 16 + t) * TILE), TILE), :] = sage_own[
                            layer, pl.ds(at, TILE), :
                        ]

    def spread_left():
        for m in range(3):
            for core in (0, 1):

                @pl.when(source_of(m, core) == g)
                def _():
                    for layer in (0, 1):
                        arrived(sage.at[layer, 0, pl.ds(0, 240)], spread_send)

                        @pl.when(c != core)
                        def _():
                            arrived(sage.at[layer, 0, pl.ds(0, TILE)], spread_send)

    def unit_ref(layer, owner):
        return sage.at[layer, :, pl.ds(aligned((c * 16 + owner) * TILE), TILE)]

    def unit_push(layer, owner, targets):
        for to in targets:
            pltpu.make_async_remote_copy(
                unit_ref(layer, owner),
                unit_ref(layer, owner),
                unit_send.at[layer],
                unit_sem.at[layer, owner],
                device_id=(to, g),
                device_id_type=MESH,
            ).start()

    def unit_wait(layer, da, db):
        owner = chip(pa + da, pb + db)
        arrived(unit_ref(layer, owner), unit_sem.at[layer, owner])
        return owner

    along_b = (chip(pa, pb + 2), b_plus, b_minus)

    def unit_start(layer):
        for m in range(3):

            @pl.when(source_of(m, c) != g)
            def _():
                arrived(tile(layer, m, c), spread_sem.at[layer, m])

        unit_push(layer, t, (chip(pa + 2, pb), a_plus, a_minus) + along_b)

    def unit_pass(layer):
        for da in (-1, 1, 2):
            unit_push(layer, unit_wait(layer, da, 0), along_b)

    def unit_end(layer):
        for db in (-1, 1, 2):
            for da in (0, -1, 1, 2):
                unit_wait(layer, da, db)
        every = sage.at[layer, :, pl.ds(aligned(c * 256), 256)]
        pltpu.make_async_remote_copy(
            every,
            every,
            pair_send.at[layer],
            pair_sem.at[layer],
            device_id=sibling,
            device_id_type=MESH,
        ).start()
        other = sage.at[layer, :, pl.ds(aligned((1 - c) * 256), 256)]
        arrived(other, pair_sem.at[layer])

    spread_out(1)
    spread_out(0)

    def wt_take(da, db, i, targets):
        row = piece_row(chip(pa + da, pb + db), i, c)
        arrived(wt_ref(row), wt_sem.at[row // PIECE])
        for to in targets:
            wt_push(row, to)
        wt_pair(row)

    def wt_near():
        wt_take(-1, 0, 0, (b_plus, b_minus, a_plus))
        wt_take(1, 0, 0, (b_plus, b_minus))
        wt_take(0, -1, 0, (b_plus,))
        wt_take(0, 1, 0, ())
        wt_take(-1, 0, 1, (b_plus, b_minus))
        wt_take(1, 0, 1, (b_plus, b_minus, a_minus))
        wt_take(0, -1, 1, ())
        wt_take(0, 1, 1, (b_minus,))

    def wt_side():
        wt_take(2, 0, 0, (b_plus, b_minus))
        wt_take(2, 0, 1, (b_plus, b_minus))
        wt_take(-1, -1, 0, (b_plus,))
        wt_take(-1, 1, 0, ())
        wt_take(1, -1, 0, (b_plus,))
        wt_take(1, 1, 0, ())

    def wt_corner():
        wt_take(-1, -1, 1, ())
        wt_take(-1, 1, 1, (b_minus,))
        wt_take(1, -1, 1, ())
        wt_take(1, 1, 1, (b_minus,))
        wt_take(2, -1, 0, (b_plus,))
        wt_take(2, 1, 0, ())
        wt_take(2, -1, 1, ())
        wt_take(2, 1, 1, (b_minus,))

    def wt_far():
        for da in (0, -1, 1, 2):
            for i in (0, 1):
                wt_take(da, 2, i, ())

    loads[4].wait()

    gain = in_gain[...].reshape(1, D)
    bias = in_bias[...].reshape(1, D)

    def norm_block(b, carry):
        rows = pl.ds(aligned(b * BLOCK), BLOCK)
        states = tok[rows, :].astype(f32)
        mean = jnp.mean(states, axis=1, keepdims=True)
        centred = states - mean
        variance = jnp.mean(centred * centred, axis=1, keepdims=True)
        normed[rows, :] = (
            centred * lax.rsqrt(variance + EPS) * gain + bias
        ).astype(bf16)
        return carry

    lax.fori_loop(0, BLOCKS, norm_block, 0)


    wt_near()

    def tile_push(src, dst, k, to, me, device):
        pltpu.make_async_remote_copy(
            src.at[pl.ds(aligned(to * TILE), TILE)],
            dst.at[pl.ds(aligned(me * TILE), TILE)],
            ex_send.at[k],
            ex_recv.at[k],
            device_id=device,
            device_id_type=MESH,
        ).start()

    def keep_own(src, dst, me):
        mine = pl.ds(aligned(me * TILE), TILE)
        dst[mine, :] = src[mine, :]

    def over_text(src, dst, k):
        for dy, dx in FAR_FIRST:
            to = (y + dy) % 4 * 4 + (x + dx) % 4
            tile_push(src, dst, k, to, t, (to, g))
        keep_own(src, dst, t)

    def over_graph(src, dst, k):
        def far_first(i, carry):
            distance = 8 + (i + 1) // 2 * (1 - i % 2 * 2)
            chip_at = (z + distance) % RING * 2
            for to in (chip_at + c, chip_at + 1 - c):
                tile_push(src, dst, k, to, g, (t, to))
            return carry

        lax.fori_loop(0, RING - 1, far_first, 0)
        tile_push(src, dst, k, z * 2 + 1 - c, g, sibling)
        keep_own(src, dst, g)

    def finish(ref, sem, k, count):
        part = ref.at[pl.ds(0, (count - 1) * TILE)]
        pltpu.make_async_copy(part, part, sem.at[k]).wait()

    owner_row = owner_text[...].astype(f32)
    owner = jnp.sum(jnp.where(iota((16, 16), 0) == iota((16, 16), 1), owner_row, 0.0), axis=1, keepdims=True)
    lane_abstract = iota((16, 96), 1) & 15
    sub_abstract = iota((16, 96), 0)
    target = jnp.sum(jnp.where(lane_abstract == sub_abstract, owner, 0.0), axis=0, keepdims=True)
    earlier = jnp.sum(
        jnp.where((sub_abstract < lane_abstract) & (owner == target), 1.0, 0.0),
        axis=0,
        keepdims=True,
    )
    slot = target * 2.0 + earlier
    r = iota((256, 96), 0)
    lane = iota((256, 96), 1)
    place = r & 15
    cap = jnp.where(place >= 6, 1, 0)
    slot_row = ((r >> 4) * 2 + cap).astype(f32)
    sj[...] = one_hot((place < 12) & (place - 6 * cap == lane >> 4) & (slot_row == slot))
    flags = one_hot(
        (place < 2) & (lane < 16) & (((r >> 4) * 2 + place).astype(f32) == slot)
    )
    flag_out[...] = mm(flags, jnp.ones((96, 128), bf16)).astype(bf16)
    over_text(flag_out, flag_in, 0)
    sjt[...] = transposed(sj[...])


    wt_side()

    wt_corner()
    unit_start(1)
    wt_far()
    unit_pass(1)
    unit_start(0)

    def wait_pair(early):
        def one(tt, carry):
            for i in (0, 1):
                row = piece_row(tt, i, 1 - c)
                wanted = row < 1536 if early else row >= 1536

                @pl.when((tt != t) & wanted)
                def _():
                    arrived(wt_ref(row), wt_sem.at[row // PIECE])

            return carry

        lax.fori_loop(0, N_TEXT, one, 0)

    wait_pair(True)

    def project(k, carry):
        cols = pl.ds(pl.multiple_of(k * 256, 256), 256)
        qk[:, cols] = mm_t(normed[...], wt[cols, :]).astype(bf16)
        return carry

    lax.fori_loop(0, 6, project, 0)

    ones = jnp.ones((BLOCK, BLOCK), bf16)
    low = iota((BLOCK, BLOCK), 1) < HEAD
    mix[...] = jnp.where(iota((16, BLOCK), 0) == HEADS, 1.0, 0.0)

    def attend(b, carry):
        rows = pl.ds(aligned(b * BLOCK), BLOCK)
        docs = doc_ids[pl.ds(b, 1), :]
        docs_here = jnp.broadcast_to(docs, (BLOCK, BLOCK)).astype(f32)
        docs_there = mm_t(eye(BLOCK), docs_here.astype(bf16))
        same = docs_here == docs_there
        same = jnp.concatenate([same, same], axis=0)
        for pair in range(HEADS // 2):
            lanes = slice(pair * 128, (pair + 1) * 128)
            q = qk[rows, lanes]
            key = qk[rows, D + pair * 128 : D + (pair + 1) * 128]
            zero = jnp.zeros_like(q)
            both = jnp.concatenate([jnp.where(low, q, zero), jnp.where(low, zero, q)], axis=0)
            scores = mm_t(both, key) * HEAD ** (-0.5)
            weights = jnp.where(same, jnp.exp(scores), 0.0)
            sums = mm(weights.astype(bf16), ones)
            probs = weights / sums
            mix[2 * pair : 2 * pair + 1, :] = jnp.sum(probs[:BLOCK], axis=0, keepdims=True)
            mix[2 * pair + 1 : 2 * pair + 2, :] = jnp.sum(probs[BLOCK:], axis=0, keepdims=True)
        heads = mix[...]
        doc_f = docs.astype(f32)
        spread = jnp.concatenate(
            [heads * jnp.where(doc_f == float(j), 1.0, 0.0) for j in range(4)], axis=0
        )
        pooled[pl.ds(aligned(b * 64), 64), :] = mm(spread.astype(bf16), normed[rows, :])
        return carry

    attend(0, 0)
    unit_pass(0)
    attend(1, 0)
    attend(2, 0)
    attend(3, 0)

    wait_pair(False)
    sums = pooled[...]
    high = sums.astype(bf16)
    rest = (sums - high.astype(f32)).astype(bf16)
    per_head = mm_t(high, wt[1536:2304, :])
    chosen = (iota((256, D), 0) & 15) == (iota((256, D), 1) >> 6)
    doc_of = iota((16, 256), 0) == (iota((16, 256), 1) >> 4)
    context = mm(one_hot(doc_of), jnp.where(chosen, per_head, 0.0).astype(bf16)).astype(bf16)
    plain = one_hot(doc_of & ((iota((16, 256), 1) & 15) == HEADS))
    pooled_norm = mm(plain, high) + mm(plain, rest)
    doc_row = iota((16, BLOCK), 0)
    docs = doc_ids[...]
    docs16 = jnp.where(
        doc_row < 8,
        jnp.where(doc_row < 4, docs[0:1, :], docs[1:2, :]),
        jnp.where(doc_row < 12, docs[2:3, :], docs[3:4, :]),
    )
    lengths = jnp.sum(jnp.where(docs16 == (doc_row & 3), 1.0, 0.0), axis=1, keepdims=True)
    total = pooled_norm + mm_t(context, wt[2304:3072, :])
    embedded = (total / lengths).astype(bf16)
    emb_out[...] = mm(sj[...], stacked(embedded)).astype(bf16)
    over_text(emb_out, emb_in, 1)

    r = iota((512, 192), 0)
    place = r & 15
    second = jnp.where(place >= 6, 1, 0)
    same_chunk = (place < 12) & (place - 6 * second == iota((512, 192), 1) >> 5)
    tile_of = one_hot(iota((32, 192), 0) == (iota((32, 192), 1) & 31))
    nbr = mm(neighbours[...].astype(f32).astype(bf16), tile_of)
    listed = iota((96, 192), 0).astype(f32)
    adj_t = jnp.zeros((96, 192), f32)
    for k in range(FAN):
        adj_t = adj_t + jnp.where(listed == nbr[k : k + 1, :], 1.0, 0.0)
    adj_t = adj_t.astype(bf16)
    r64 = iota((512, 64), 0)
    place64 = r64 & 15
    halo_of = one_hot(
        (place64 < 12)
        & ((r64 >> 4) * 2 + jnp.where(place64 >= 6, 1, 0) == iota((512, 64), 1))
    )
    aj[...] = jnp.where(same_chunk, mm(halo_of, adj_t[32:96, :]), 0.0).astype(bf16)
    ajt[...] = transposed(aj[...])
    own_adj_t = adj_t[0:32, 0:32]
    own_adj = transposed(own_adj_t)
    node_lane = iota((32, 192), 1) & 31
    bnd = mm_t(eye(32), boundary[...].astype(f32).astype(bf16))
    node_lane_f = node_lane.astype(f32)
    r32 = iota((512, 32), 0)
    place32 = r32 & 15
    peer32 = (r32 >> 4) == iota((512, 32), 1)
    picked = mm(one_hot(peer32 & (place32 < 6)), one_hot(bnd[:, 0:1] == node_lane_f)) + mm(
        one_hot(peer32 & (place32 >= 6) & (place32 < 12)), one_hot(bnd[:, 1:2] == node_lane_f)
    )
    pj[...] = jnp.where(same_chunk, picked, 0.0).astype(bf16)
    pjt[...] = transposed(pj[...])
    n = iota((192, 256), 0)
    m = iota((192, 256), 1)
    uj = one_hot(((m >> 4) == (n & 31) >> 1) & ((m & 15) == (n & 1) * 6 + (n >> 5)))
    m = iota((256, 192), 0)
    n = iota((256, 192), 1)
    ujt = one_hot(((m >> 4) == (n & 31) >> 1) & ((m & 15) == (n & 1) * 6 + (n >> 5)))


    unit_end(1)
    finish(flag_in, ex_recv, 0, N_TEXT)
    live = mm(
        one_hot(
            ((iota((32, 256), 1) >> 4) == (iota((32, 256), 0) >> 1))
            & ((iota((32, 256), 1) & 15) == (iota((32, 256), 0) & 1))
        ),
        flag_in[...],
    )[:, 0:1]
    loads[5].wait()

    def lower(v, layer):
        return mm(v[:, :512], sage[layer, 0]) + mm(v[:, 512:], sage[layer, 1, 0:256, :])

    def upper(v, layer):
        return mm(v[:, :256], sage[layer, 1, 256:512, :]) + mm(v[:, 256:], sage[layer, 2])

    def lower_t(u, layer):
        return jnp.concatenate(
            [mm_t(u, sage[layer, 0]), mm_t(u, sage[layer, 1, 0:256, :])], axis=1
        )

    def spread_of(u, layer):
        back = jnp.concatenate(
            [mm_t(u, sage[layer, 1, 256:512, :]), mm_t(u, sage[layer, 2])], axis=1
        )
        return (back / FAN).astype(bf16)

    def send_back(spread, dst_out, dst_in, k):
        dst_out[...] = mm(aj[...], stacked(spread)).astype(bf16)
        over_graph(dst_out, dst_in, k)

    grad_two = (live * grad_in[...].astype(f32)).astype(bf16)
    spread_two = spread_of(grad_two, 1)
    send_back(spread_two, back_two_out, back_two_in, 2)
    finish(emb_in, ex_recv, 1, N_TEXT)
    v_stack = mm(uj, emb_in[...]).astype(bf16)
    one_out[...] = mm(pj[...], v_stack).astype(bf16)
    over_graph(one_out, one_in, 3)
    v = unstacked(v_stack)
    into_one = lower_t(grad_two, 1) + mm(own_adj_t, spread_two)
    own_part = mm(own_adj, v)
    unit_end(0)
    preact = lower(v, 0)
    finish(back_two_in, ex_recv, 2, N_GRAPH)
    into_one = into_one + unstacked(mm(pjt[...], back_two_in[...]))

    finish(one_in, ex_recv, 3, N_GRAPH)
    aggregated = ((own_part + unstacked(mm(ajt[...], one_in[...]))) / FAN).astype(bf16)
    preact = preact + upper(aggregated, 0)
    slope = 0.7978845608028654
    squared = preact * preact
    bent = jnp.tanh(slope * (preact + 0.044715 * squared * preact))
    hidden = (live * (0.5 * preact * (1.0 + bent))).astype(bf16)
    steep = 0.5 * (1.0 + bent) + 0.5 * preact * (1.0 - bent * bent) * (
        slope * (1.0 + 3.0 * 0.044715 * squared)
    )
    grad_one = (live * steep * into_one).astype(bf16)
    spread_one = spread_of(grad_one, 0)
    send_back(spread_one, back_one_out, back_one_in, 4)
    two_out[...] = mm(pj[...], stacked(hidden)).astype(bf16)
    over_graph(two_out, two_in, 5)
    embed_grad = lower_t(grad_one, 0) + mm(own_adj_t, spread_one)
    preact_two = lower(hidden, 1)
    own_two = mm(own_adj, hidden)

    finish(back_one_in, ex_recv, 4, N_GRAPH)
    embed_grad = (embed_grad + unstacked(mm(pjt[...], back_one_in[...]))).astype(bf16)
    ret_out[...] = mm(ujt, stacked(embed_grad)).astype(bf16)
    over_text(ret_out, ret_in, 6)

    finish(two_in, ex_recv, 5, N_GRAPH)
    aggregated = ((own_two + unstacked(mm(ajt[...], two_in[...]))) / FAN).astype(bf16)
    preact_two = preact_two + upper(aggregated, 1)
    node_states[...] = (live * preact_two).astype(bf16)

    finish(ret_in, ex_recv, 6, N_TEXT)
    abstract_grad[...] = unstacked(mm(sjt[...], ret_in[...]).astype(bf16))

    arrived(wt.at[pl.ds(0, 30 * PIECE)], wt_send)
    arrived(wt.at[pl.ds(0, 30 * PIECE)], wt_pair_send)
    spread_left()
    for layer in (0, 1):
        arrived(sage.at[layer, :, pl.ds(0, 240)], unit_send.at[layer])
        arrived(sage.at[layer, :, pl.ds(0, 256)], pair_send.at[layer])
    for k, (ref, count) in enumerate(
        (
            (flag_out, N_TEXT),
            (emb_out, N_TEXT),
            (back_two_out, N_GRAPH),
            (one_out, N_GRAPH),
            (back_one_out, N_GRAPH),
            (two_out, N_GRAPH),
            (ret_out, N_TEXT),
        )
    ):
        finish(ref, ex_send, k, count)


def local(
    tokens,
    doc_ids,
    in_gain,
    in_bias,
    attn_qkv,
    attn_out,
    owner_text,
    sage_one,
    sage_two,
    neighbours,
    boundary,
    out_grad,
):
    anywhere = pl.BlockSpec(memory_space=pl.ANY)
    vmem = pl.BlockSpec(memory_space=pltpu.VMEM)
    text_tiles = pltpu.VMEM((N_TEXT * TILE, 128), bf16)
    graph_tiles = pltpu.VMEM((N_GRAPH * TILE, 128), bf16)
    return pl.pallas_call(
        kernel,
        out_shape=(
            jax.ShapeDtypeStruct((ROWS, D), bf16),
            jax.ShapeDtypeStruct((16, D), bf16),
        ),
        in_specs=[anywhere] * 6 + [vmem] * 6,
        out_specs=(vmem, vmem),
        scratch_shapes=[
            pltpu.VMEM((512, D), bf16),
            pltpu.VMEM((ROWS, D), bf16),
            pltpu.VMEM((3072, D), bf16),
            pltpu.VMEM((2, PIECE, D), bf16),
            pltpu.VMEM((2, 3, 512, D), bf16),
            pltpu.VMEM((512, D), bf16),
            pltpu.VMEM((512, 2 * D), bf16),
            pltpu.VMEM((256, D), f32),
            pltpu.VMEM((16, BLOCK), f32),
            pltpu.VMEM((16, BLOCK), f32),
            pltpu.VMEM((512, 192), bf16),
            pltpu.VMEM((192, 512), bf16),
            pltpu.VMEM((512, 192), bf16),
            pltpu.VMEM((192, 512), bf16),
            pltpu.VMEM((256, 96), bf16),
            pltpu.VMEM((96, 256), bf16),
            text_tiles,
            text_tiles,
            text_tiles,
            text_tiles,
            graph_tiles,
            graph_tiles,
            graph_tiles,
            graph_tiles,
            graph_tiles,
            graph_tiles,
            graph_tiles,
            graph_tiles,
            text_tiles,
            text_tiles,
            pltpu.SemaphoreType.DMA((6,)),
            pltpu.SemaphoreType.DMA((64,)),
            pltpu.SemaphoreType.DMA,
            pltpu.SemaphoreType.DMA,
            pltpu.SemaphoreType.DMA,
            pltpu.SemaphoreType.DMA((2, 3)),
            pltpu.SemaphoreType.DMA((2,)),
            pltpu.SemaphoreType.DMA((2, N_TEXT)),
            pltpu.SemaphoreType.DMA((2,)),
            pltpu.SemaphoreType.DMA((2,)),
            pltpu.SemaphoreType.DMA((7,)),
            pltpu.SemaphoreType.DMA((7,)),
        ],
        compiler_params=pltpu.CompilerParams(
            collective_id=0, has_side_effects=True, vmem_limit_bytes=56 * 1024 * 1024
        ),
    )(
        tokens,
        attn_qkv.T,
        attn_out.T,
        sage_one,
        sage_two,
        out_grad,
        doc_ids,
        in_gain,
        in_bias,
        owner_text.T,
        neighbours.T,
        boundary.T,
    )


def solution(mesh):
    split = P(("text", "graph"), None)
    return jax.shard_map(
        local,
        mesh=mesh,
        in_specs=(
            split,
            split,
            P(None),
            P(None),
            P(None, "text"),
            P(None, "text"),
            split,
            P("graph", None),
            P("graph", None),
            split,
            split,
            split,
        ),
        out_specs=(split, split),
        check_vma=False,
    )
```

time: 106 us -> 87.9 us (0.83)
  Pallas kernels: 97.9 us -> 84.9 us
  local copies, waits for them, and re-layouts: 7.29 us -> 2.04 us
    pallas_call x1, Pallas kernels: 97.9 us -> 84.9 us  [local(): pl.pallas_call(kernel, out_shape=(jax.ShapeDtypeStruct((ROWS, D), bf16),...]
    unnamed x19 -> x4, local copies, waits for them, and re-layouts: 6.52 us -> 2.04 us
where the time goes in v2:
time: 87.9 us; the launch traced here: 87.6 us
  Pallas kernels  84.9 us (97%)
  local copies, waits for them, and re-layouts  2.04 us (2%)
    pallas_call x1, Pallas kernels, local(): pl.pallas_call(kernel, out_shape=(jax.ShapeDtypeStruct((ROWS, D), bf16),...  84.9 us
    unnamed x4, local copies, waits for them, and re-layouts  2.04 us

profile of v2, /device:TPU:1, one launch (start us, length us, event | category | flops | bytes accessed | tf_op | source)
XLA Modules:
  0.0 87.6 jit_solution(6487266224950980195)
XLA Ops:
  0.6 84.9 %shard_map.131 = (bf16[32,768]{1,0:T(8,128)(2,1)}, bf16[16,768]{1,0:T(8,128)(2,1)}) custom-call(bf16[512,768]{1,0:T(8,128)(2,1)} %tokens.1, bf16[144,768]{1,0:T(8,128)(2,1)} %bitcast.5, bf16[48,768]{1,0:T(8,128)(2,1)} %bitcast.6, bf16[48,768]{1,0:T(8,128)(2,1)} %sage_one.1, bf16[48,768]{1,0:T(8,128)(2,1)} %sage_two.1, bf16[32,768]{1,0:T(8,128)(2,1)} %out_grad.1, ...), custom_call_target="tpu_custom_call" | custom-call | tf_op jit(solution)/shard_map/pallas_call | solution.py:687
  85.6 0.0 copy-start
  85.6 1.4 %copy.16 = bf16[32,768]{1,0:T(8,128)(2,1)} copy(bf16[32,768]{1,0:T(8,128)(2,1)} %get-tuple-element.4) | data formatting | bytes 98304
  87.0 0.0 copy-done
  87.0 0.6 copy.17
Async XLA Ops:
  85.6 1.4 %copy-start = (bf16[16,768]{1,0:T(8,128)(2,1)S(1)}, bf16[16,768]{1,0:T(8,128)(2,1)}, u32[]{:S(2)}) copy-start(bf16[16,768]{1,0:T(8,128)(2,1)} %get-tuple-element.5) | copy-start | bytes 73732

commit v3 on v2

--- a/solution.py
+++ b/solution.py
@@ -687,8 +687,8 @@
     return pl.pallas_call(
         kernel,
         out_shape=(
-            jax.ShapeDtypeStruct((ROWS, D), bf16),
-            jax.ShapeDtypeStruct((16, D), bf16),
+            pltpu.VMEM((ROWS, D), bf16),
+            pltpu.VMEM((16, D), bf16),
         ),
         in_specs=[anywhere] * 6 + [vmem] * 6,
         out_specs=(vmem, vmem),

time: 87.9 us -> 86.3 us (0.982)
    unnamed x4 -> x2, local copies, waits for them, and re-layouts: 2.04 us -> 1.23 us
where the time goes in v3:
time: 86.3 us; the launch traced here: 86.1 us
  Pallas kernels  84.2 us (98%)
  local copies, waits for them, and re-layouts  1.23 us (1%)
    pallas_call x1, Pallas kernels, local(): pl.pallas_call(kernel, out_shape=(pltpu.VMEM((ROWS, D), bf16), pltpu.VMEM...  84.2 us

profile of v3, /device:TPU:1, one launch (start us, length us, event | category | flops | bytes accessed | tf_op | source)
XLA Modules:
  0.0 86.1 jit_solution(12597090396386047804)
XLA Ops:
  0.6 84.2 %shard_map.131 = (bf16[32,768]{1,0:T(8,128)(2,1)S(1)}, bf16[16,768]{1,0:T(8,128)(2,1)S(1)}) custom-call(bf16[512,768]{1,0:T(8,128)(2,1)} %tokens.1, bf16[144,768]{1,0:T(8,128)(2,1)} %bitcast.5, bf16[48,768]{1,0:T(8,128)(2,1)} %bitcast.6, bf16[48,768]{1,0:T(8,128)(2,1)} %sage_one.1, bf16[48,768]{1,0:T(8,128)(2,1)} %sage_two.1, bf16[32,768]{1,0:T(8,128)(2,1)} %out_grad.1, ...), custom_call_target="tpu_custom_call" | custom-call | tf_op jit(solution)/shard_map/pallas_call | solution.py:687
  84.9 0.6 copy.16
  85.5 0.6 copy.17

commit v4 on v3

--- a/solution.py
+++ b/solution.py
@@ -139,10 +139,10 @@
         return carry
 
     def greet_graph(i, carry):
-        pl.semaphore_signal(barrier, inc=1, device_id=(t, (g + i) % N_GRAPH), device_id_type=MESH)
+        pl.semaphore_signal(barrier, inc=1, device_id=(t, (g + 16 + (i + 1) // 2 * (1 - i % 2 * 2)) % N_GRAPH), device_id_type=MESH)
         return carry
 
-    lax.fori_loop(1, N_GRAPH, greet_graph, 0)
+    lax.fori_loop(0, N_GRAPH - 1, greet_graph, 0)
     lax.fori_loop(1, N_TEXT, greet_text, 0)
 
     own_qkv = wt.at[pl.ds(aligned(t * 144), 144)]
@@ -410,6 +410,28 @@
     def finish(ref, sem, k, count):
         part = ref.at[pl.ds(0, (count - 1) * TILE)]
         pltpu.make_async_copy(part, part, sem.at[k]).wait()
+
+    wt_side()
+
+    wt_corner()
+    unit_start(1)
+    wt_far()
+    unit_pass(1)
+    unit_start(0)
+
+    def wait_pair(early):
+        def one(tt, carry):
+            for i in (0, 1):
+                row = piece_row(tt, i, 1 - c)
+                wanted = row < 1536 if early else row >= 1536
+
+                @pl.when((tt != t) & wanted)
+                def _():
+                    arrived(wt_ref(row), wt_sem.at[row // PIECE])
+
+            return carry
+
+        lax.fori_loop(0, N_TEXT, one, 0)
 
     owner_row = owner_text[...].astype(f32)
     owner = jnp.sum(jnp.where(iota((16, 16), 0) == iota((16, 16), 1), owner_row, 0.0), axis=1, keepdims=True)
@@ -435,28 +457,6 @@
     over_text(flag_out, flag_in, 0)
     sjt[...] = transposed(sj[...])
 
-
-    wt_side()
-
-    wt_corner()
-    unit_start(1)
-    wt_far()
-    unit_pass(1)
-    unit_start(0)
-
-    def wait_pair(early):
-        def one(tt, carry):
-            for i in (0, 1):
-                row = piece_row(tt, i, 1 - c)
-                wanted = row < 1536 if early else row >= 1536
-
-                @pl.when((tt != t) & wanted)
-                def _():
-                    arrived(wt_ref(row), wt_sem.at[row // PIECE])
-
-            return carry
-
-        lax.fori_loop(0, N_TEXT, one, 0)
 
     wait_pair(True)
 

time: 86.3 us -> 86.5 us (level)
  no operation moved by 1% of the time
where the time goes in v4:
time: 86.5 us; the launch traced here: 86.3 us
  Pallas kernels  84.4 us (98%)
  local copies, waits for them, and re-layouts  1.23 us (1%)
    pallas_call x1, Pallas kernels, local(): pl.pallas_call(kernel, out_shape=(pltpu.VMEM((ROWS, D), bf16), pltpu.VMEM...  84.4 us

profile of v4, /device:TPU:1, one launch (start us, length us, event | category | flops | bytes accessed | tf_op | source)
XLA Modules:
  0.0 86.3 jit_solution(8461325669284346274)
XLA Ops:
  0.6 84.4 %shard_map.131 = (bf16[32,768]{1,0:T(8,128)(2,1)S(1)}, bf16[16,768]{1,0:T(8,128)(2,1)S(1)}) custom-call(bf16[512,768]{1,0:T(8,128)(2,1)} %tokens.1, bf16[144,768]{1,0:T(8,128)(2,1)} %bitcast.5, bf16[48,768]{1,0:T(8,128)(2,1)} %bitcast.6, bf16[48,768]{1,0:T(8,128)(2,1)} %sage_one.1, bf16[48,768]{1,0:T(8,128)(2,1)} %sage_two.1, bf16[32,768]{1,0:T(8,128)(2,1)} %out_grad.1, ...), custom_call_target="tpu_custom_call" | custom-call | tf_op jit(solution)/shard_map/pallas_call | solution.py:687
  85.1 0.6 copy.16
  85.7 0.6 copy.17
